TPU v7x, 512 devices: a whole 4x8x8 slice. The times are simulated.
512 devices in a mesh: row: 8 (over z_lo, core), col: 16 (over y, z_hi), depth: 4 (over x).
Axes of the slice: x: 4, y: 8, z: 8 (z_hi: 2, z_lo: 4; z = z_hi * 4 + z_lo), core: 2. Of those that a mesh axis runs over, the one named last changes fastest.
Arguments:
- adjoint_slab: bfloat16 [12288, 65536], P('row', ('col', 'depth')), may hold values from -16 to 16
- panel_cols: bfloat16 [65536, 512], P(('col', 'depth'), 'row'), may hold values from -0.0234375 to 0.0234375
- incoming: float32 [12288, 512], P(('row', 'col', 'depth')), may hold values from -6 to 6
- inverse_block: float32 [512, 512], replicated, may hold values from -0.2 to 2, as said below
- panel_rows: bfloat16 [12288, 512], P(('row', 'col', 'depth')), may hold values from -0.0546875 to 0.0546875
Outputs:
- grad_rows: float32 [12288, 512], P(('row', 'col', 'depth'))
- panel_term: float32 [512, 512], replicated
Inputs may be any that keep to these rules, and one draw needn't show every extreme that they name: inverse_block is lower triangular with diagonal between 1 and 2.
All inputs are finite; a program needn't handle non-finite values.
Results may differ from a plain program's by a relative error of at most 0.0003.
Values may be sent and summed in bfloat16 or wider, within the bound.
A program may use at most 64 MiB of HBM per device.

v0:
```python
import jax
import jax.numpy as jnp
from jax import lax
from jax.sharding import PartitionSpec as P


def on_device(adjoint_slab, panel_cols, incoming, inverse_block, panel_rows):
    whole_panel = lax.all_gather(panel_cols, "row", axis=1, tiled=True)
    partial_value = lax.psum_scatter(
        jnp.dot(adjoint_slab, whole_panel, preferred_element_type=jnp.float32),
        ("col", "depth"),
        scatter_dimension=0,
        tiled=True,
    )
    panel_adjoint = incoming - 2.0 * partial_value
    gradient = jnp.dot(panel_adjoint, inverse_block, precision=lax.Precision.HIGHEST)
    contrib = jnp.dot(
        panel_rows.astype(jnp.float32).T, panel_adjoint, precision=lax.Precision.HIGHEST
    )
    summed = lax.psum(contrib, ("row", "col", "depth"))
    return (gradient, summed)


def solution(mesh):
    return jax.shard_map(
        on_device,
        mesh=mesh,
        in_specs=(
            P("row", ("col", "depth")),
            P(("col", "depth"), "row"),
            P(("row", "col", "depth"), None),
            P(),
            P(("row", "col", "depth"), None),
        ),
        out_specs=(P(("row", "col", "depth"), None), P()),
        check_vma=False,
    )
```

profile of v0, /device:TPU:1, one launch (start us, length us, event | category | flops | bytes accessed | tf_op | source)
XLA Modules:
  0.0 1170.5 jit_solution(11256195326988512245)
XLA Ops:
  7.2 0.0 copy-start
  7.2 0.0 all-gather.2.cloned.1.call-start
  7.2 0.7 all-gather.2.cloned.1.call-update
  7.9 0.0 reduce-scatter.2.cloned.1.call-start
  8.0 45.5 %all-gather.2.cloned.1.call-done = bf16[1024,512]{0,1:T(8,128)(2,1)} async-done(((bf16[1024,64]{0,1:T(8,128)(2,1)}), bf16[1024,512]{0,1:T(8,128)(2,1)}) %all-gather.2.cloned.1.call-update) | async-done | bytes 1048592 | tf_op jit(solution)/shard_map/all_gather | solution.py:8
  53.5 0.0 copy-done
  53.5 4.7 fusion.3
  58.2 0.0 copy-start.1
  58.2 0.0 copy-start.2
  58.2 0.0 reduce-scatter.2.cloned.1.call-update
  58.2 0.0 all-reduce.2.cloned.1.call-start
  58.3 825.4 %reduce-scatter.2.cloned.1.call-done = f32[24,512]{1,0:T(8,128)} async-done(((f32[1536,512]{1,0:T(8,128)}), f32[24,512]{1,0:T(8,128)}) %reduce-scatter.2.cloned.1.call-update) | async-done | bytes 49168 | tf_op jit(solution)/shard_map/reduce_scatter | solution.py:9
  883.7 0.0 copy-done.1
  883.7 0.0 copy-done.2
  883.7 2.4 convolution_bitcast_fusion
  886.1 0.0 all-reduce.2.cloned.1.call-update
  886.1 2.5 fusion
  888.6 272.8 %all-reduce.2.cloned.1.call-done = f32[512,512]{0,1:T(8,128)} async-done(((f32[512,512]{0,1:T(8,128)}), f32[512,512]{0,1:T(8,128)}) %all-reduce.2.cloned.1.call-update) | async-done | bytes 1048592 | tf_op jit(solution)/shard_map/psum | solution.py:20
  1161.4 2.5 copy.7
Async XLA Ops:
  7.2 46.3 %copy-start = (bf16[1536,1024]{1,0:T(8,128)(2,1)S(1)}, bf16[1536,1024]{1,0:T(8,128)(2,1)}, u32[]{:S(2)}) copy-start(bf16[1536,1024]{1,0:T(8,128)(2,1)} %param.5) | copy-start | bytes 9437188
  7.2 46.3 %all-gather.2.cloned.1.call-start = ((), (), s32[]{:S(2)}) async-start(), calls=%async_computation.1 | async-start | bytes 1179648 | tf_op jit(solution)/shard_map/all_gather | solution.py:8
  7.9 875.8 %reduce-scatter.2.cloned.1.call-start = ((), (), s32[]{:S(2)}) async-start(), calls=%async_computation.2 | async-start | bytes 3194880 | tf_op jit(solution)/shard_map/reduce_scatter | solution.py:9
  58.2 825.5 %copy-start.1 = (f32[24,512]{1,0:T(8,128)S(1)}, f32[24,512]{1,0:T(8,128)}, u32[]{:S(2)}) copy-start(f32[24,512]{1,0:T(8,128)} %param.7) | copy-start | bytes 147460
  58.2 825.5 %copy-start.2 = (bf16[24,512]{1,0:T(8,128)(2,1)S(1)}, bf16[24,512]{1,0:T(8,128)(2,1)}, u32[]{:S(2)}) copy-start(bf16[24,512]{1,0:T(8,128)(2,1)} %param.9) | copy-start | bytes 73732
  58.2 1103.2 %all-reduce.2.cloned.1.call-start = ((), (), s32[]{:S(2)}) async-start(), calls=%async_computation.3 | async-start | bytes 2097152 | tf_op jit(solution)/shard_map/psum | solution.py:20
Sparse Core Ops, SparseCore 0:
  10.1 43.3 all-gather.1
  59.9 823.7 reduce-scatter.1
  889.3 272.0 all-reduce.1
where the time goes:
time: 1170 us
  waiting for transfers between devices  1140 us (97%)
  between operations  13.8 us (1%)
    reduce_scatter x1, waiting for transfers between devices, on_device(): lax.psum_scatter(jnp.dot(adjoint_slab, whole_panel, preferred_element_typ...  825 us
    psum x1, waiting for transfers between devices, on_device(): summed = lax.psum(contrib, ('row', 'col', 'depth'))  273 us
    all_gather x1, waiting for transfers between devices, on_device(): whole_panel = lax.all_gather(panel_cols, 'row', axis=1, tiled=True)  45.5 us
  transfers between devices with their start and end apart: 3, of which 3 were waited for; matrix products, arithmetic and copies ran while one was open for 0% of the time, Pallas kernels for 0%

commit v1 on v0

v1 whole, which is shorter than its diff:
```python
import jax
import jax.numpy as jnp
from jax import lax
from jax.experimental import pallas as pl
from jax.experimental.pallas import tpu as pltpu
from jax.sharding import PartitionSpec as P

MESH = pl.DeviceIdType.MESH
F32, BF16 = jnp.float32, jnp.bfloat16
STEPS = 250.0
HALF = 125.0
COPIES = 96


def encode(value):
    groups = value.reshape(-1, 8, 128)
    size = jnp.abs(groups)
    scale = jnp.maximum(jnp.max(size, axis=0) * 1.004, 1e-30).astype(BF16)
    power = jnp.exp2(size * (STEPS / scale.astype(F32)) - HALF)
    code = jnp.where(groups < 0.0, -power, power).reshape(value.shape)
    scale = scale.astype(F32)
    return jnp.concatenate([code, scale, scale], axis=0).astype(BF16)


def decode(coded):
    coded = coded.astype(F32)
    rows = coded.shape[0] - 16
    groups = coded[:rows].reshape(-1, 8, 128)
    scale = coded[rows : rows + 8] * (1.0 / STEPS)
    steps = jnp.log2(jnp.abs(groups)) + HALF
    return (jnp.where(groups < 0.0, -steps, steps) * scale).reshape(rows, 128)


def kernel(
    a_hbm, b_ref, inc_ref, inv_hbm, p_ref,
    grad_ref, term_ref,
    a, inv, b_sib, b_all, own, xs, xr, ys, yr, ysum, tz, tzr, tx, p_all, p_mat,
    half, half_r, slab, slab_r, zsum, ysl, coded, local_sem, send_sem, recv_sem,
):
    row, col, x = lax.axis_index("row"), lax.axis_index("col"), lax.axis_index("depth")
    zl, c = lax.div(row, 2), lax.rem(row, 2)
    y, zh = lax.div(col, 2), lax.rem(col, 2)
    z = zh * 4 + zl

    def at(x=x, y=y, zh=zh, zl=zl, c=c):
        return (zl * 2 + c, y * 2 + zh, x)

    def x_peer(d):
        return at(x=lax.rem(x + d, 4))

    def y_peer(d):
        return at(y=lax.rem(y + d, 8))

    def z_peer(d):
        other = lax.rem(z + d, 8)
        return at(zh=lax.div(other, 4), zl=lax.rem(other, 4))

    sibling = at(c=1 - c)
    z_far = at(zh=1 - zh)

    load_a = pltpu.make_async_copy(a_hbm, a, local_sem.at[0])
    load_a.start()
    load_inv = pltpu.make_async_copy(inv_hbm, inv, local_sem.at[1])
    load_inv.start()

    barrier = pltpu.get_barrier_semaphore()
    peers = [sibling] + [x_peer(d) for d in range(1, 4)]
    peers += [y_peer(d) for d in range(1, 8)] + [z_peer(d) for d in range(1, 8)]
    for peer in peers:
        pl.semaphore_signal(barrier, inc=1, device_id=peer, device_id_type=MESH)

    wide = jnp.concatenate([p_ref[:, :256].astype(F32), p_ref[:, 256:].astype(F32)], axis=0)
    p_all[x, zh] = wide.astype(BF16)
    pl.semaphore_wait(barrier, len(peers))

    copies = []

    def send(src, dst, target):
        i = len(copies)
        copy = pltpu.make_async_remote_copy(
            src_ref=src, dst_ref=dst, send_sem=send_sem.at[i], recv_sem=recv_sem.at[i],
            device_id=target, device_id_type=MESH,
        )
        copy.start()
        copies.append(copy)
        return copy

    sib = send(b_ref, b_sib, sibling)
    p_far = send(p_all.at[x, zh], p_all.at[x, zh], z_far)
    sib.wait_recv()

    @pl.when(c == 0)
    def _():
        b_all[zl] = jnp.concatenate([b_ref[...], b_sib[...]], axis=1)

    @pl.when(c == 1)
    def _():
        b_all[zl] = jnp.concatenate([b_sib[...], b_ref[...]], axis=1)

    chunk = [zl, zl + 1 - 2 * lax.rem(zl, 2), lax.rem(zl + 2, 4), 3 - zl]
    mine = pl.ds(pl.multiple_of(c * 512, 512), 512)
    line = [None] * 4
    for k in range(1, 4):
        line[k] = send(b_all.at[zl, mine], b_all.at[zl, mine], at(zl=chunk[k]))

    load_a.wait()
    x_copies = [[None] * 4 for _ in range(4)]
    y_copies = [[None] * 8 for _ in range(4)]

    def multiply(k):
        for part in range(2):
            acc = jnp.dot(a[part * 768 : part * 768 + 768, :], b_all[chunk[k]], preferred_element_type=F32)
            for yy in range(4):
                for to in range(4):
                    low = yy * 192 + to * 24
                    own[k, to, (part * 4 + yy) * 48 : (part * 4 + yy) * 48 + 24, :] = acc[low : low + 24]
                    own[k, to, (part * 4 + yy) * 48 + 24 : (part * 4 + yy) * 48 + 48, :] = acc[low + 96 : low + 120]
        for d in (2, 1, 3):
            xs[k, d - 1] = encode(own[k, lax.rem(x + d, 4)])
            x_copies[k][d] = send(xs.at[k, d - 1], xr.at[k, d - 1], x_peer(d))

    def reduce_x(k):
        total = own[k, x]
        for d in (1, 3, 2):
            x_copies[k][d].wait_recv()
            total = total + decode(xr[k, d - 1])
        ysum[k] = total.reshape(8, 48, 128)
        for d in (4, 3, 5, 2, 6, 1, 7):
            ys[k, d - 1] = encode(ysum[k, lax.rem(y + d, 8)])
            y_copies[k][d] = send(ys.at[k, d - 1], yr.at[k, d - 1], y_peer(d))

    def reduce_y(k):
        total = ysum[k, y]
        for d in (1, 7, 2, 6, 3, 5, 4):
            y_copies[k][d].wait_recv()
            total = total + decode(yr[k, d - 1])
        for h in range(2):
            tz[h, chunk[k]] = total[h * 24 : h * 24 + 24] * -2.0

    multiply(0)
    p_far.wait_recv()
    p_copies = [send(p_all.at[x], p_all.at[x], x_peer(d)) for d in range(1, 4)]
    for k in range(1, 4):
        line[k].wait_recv()
        there = b_all.at[chunk[k], mine]
        forward = send(there, there, sibling)
        if k >= 2:
            reduce_x(k - 2)
        forward.wait_recv()
        multiply(k)
    reduce_x(2)
    reduce_y(0)
    reduce_y(1)
    for copy in p_copies:
        copy.wait_recv()
    for i in range(4):
        both = p_all[i].astype(F32)
        rows = [jnp.concatenate([both[h, :24], both[h, 24:]], axis=1) for h in range(2)]
        p_mat[i * 48 : i * 48 + 48, :] = jnp.concatenate(rows, axis=0).astype(BF16)
    reduce_x(3)
    reduce_y(2)
    reduce_y(3)

    far = send(tz.at[1 - zh], tzr, z_far)
    for i in range(4):
        block = inc_ref[:, i * 128 : i * 128 + 128]
        for h in range(2):
            tx[x, i, h * 24 : h * 24 + 24, :] = tz[h, i] + jnp.where(zh == h, block, 0.0)
    t_copies = []
    for d in range(1, 4):
        to = lax.rem(x + d, 4)
        t_copies.append(send(tx.at[x, to], tx.at[x, to], x_peer(d)))
    for copy in t_copies:
        copy.wait_recv()
    blocks = jnp.concatenate([tx[i, x] for i in range(4)], axis=0)
    high = blocks.astype(BF16)
    rest = blocks - high.astype(F32)
    middle = rest.astype(BF16)
    low = (rest - middle.astype(F32)).astype(BF16)
    contrib = jnp.zeros((512, 128), F32)
    for piece in (low, middle, high):
        contrib = contrib + lax.dot_general(p_mat[...], piece, (((0,), (0,)), ((), ())), preferred_element_type=F32)
    half[...] = contrib.reshape(2, 256, 128)
    swap = send(half.at[1 - c], half_r, sibling)

    load_inv.wait()
    far.wait_recv()
    adjoint = jnp.concatenate([tz[zh, i] + tzr[i] for i in range(4)], axis=1) + inc_ref[...]
    swap.wait_recv()
    slab[...] = (half[c] + half_r[...]).reshape(8, 32, 128)
    s_copies = [None] * 8
    for d in (4, 3, 5, 2, 6, 1, 7):
        s_copies[d] = send(slab.at[lax.rem(y + d, 8)], slab_r.at[d - 1], y_peer(d))
    grad_ref[...] = jnp.dot(adjoint, inv[...], precision=lax.Precision.HIGHEST, preferred_element_type=F32)
    total = slab[y]
    for d in (1, 7, 2, 6, 3, 5, 4):
        s_copies[d].wait_recv()
        total = total + slab_r[d - 1]
    zsum[z] = total
    s_copies = [send(zsum.at[z], zsum.at[z], z_peer(d)) for d in (4, 3, 5, 2, 6, 1, 7)]
    for copy in s_copies:
        copy.wait_recv()
    ysl[y] = jnp.sum(zsum[...], axis=0)
    s_copies = [send(ysl.at[y], ysl.at[y], y_peer(d)) for d in (4, 3, 5, 2, 6, 1, 7)]
    for copy in s_copies:
        copy.wait_recv()
    coded[c, x] = encode(ysl[...].reshape(256, 128))
    s_copies = [send(coded.at[c, x], coded.at[c, x], x_peer(d)) for d in (2, 1, 3)]
    last = [send(coded.at[c, x], coded.at[c, x], sibling)]
    for copy, d in zip((s_copies[1], s_copies[2], s_copies[0]), (1, 3, 2)):
        copy.wait_recv()
        source = lax.rem(x - d + 4, 4)
        last.append(send(coded.at[c, source], coded.at[c, source], sibling))
    for copy in last:
        copy.wait_recv()
    term_ref[...] = coded[...]
    for copy in copies:
        copy.wait_send()


def on_device(adjoint_slab, panel_cols, incoming, inverse_block, panel_rows):
    vmem, hbm = pl.BlockSpec(memory_space=pltpu.VMEM), pl.BlockSpec(memory_space=pl.ANY)
    gradient, coded = pl.pallas_call(
        kernel,
        name="panel",
        out_shape=(
            jax.ShapeDtypeStruct((24, 512), F32),
            jax.ShapeDtypeStruct((2, 4, 272, 128), BF16),
        ),
        in_specs=[hbm, vmem, vmem, hbm, vmem],
        out_specs=(vmem, vmem),
        scratch_shapes=[
            pltpu.VMEM((1536, 1024), BF16),
            pltpu.VMEM((512, 512), F32),
            pltpu.VMEM((1024, 64), BF16),
            pltpu.VMEM((4, 1024, 128), BF16),
            pltpu.VMEM((4, 4, 384, 128), F32),
            pltpu.VMEM((4, 3, 400, 128), BF16),
            pltpu.VMEM((4, 3, 400, 128), BF16),
            pltpu.VMEM((4, 7, 64, 128), BF16),
            pltpu.VMEM((4, 7, 64, 128), BF16),
            pltpu.VMEM((4, 8, 48, 128), F32),
            pltpu.VMEM((2, 4, 24, 128), F32),
            pltpu.VMEM((4, 24, 128), F32),
            pltpu.VMEM((4, 4, 48, 128), F32),
            pltpu.VMEM((4, 2, 48, 256), BF16),
            pltpu.VMEM((192, 512), BF16),
            pltpu.VMEM((2, 256, 128), F32),
            pltpu.VMEM((256, 128), F32),
            pltpu.VMEM((8, 32, 128), F32),
            pltpu.VMEM((7, 32, 128), F32),
            pltpu.VMEM((8, 32, 128), F32),
            pltpu.VMEM((8, 32, 128), F32),
            pltpu.VMEM((2, 4, 272, 128), BF16),
            pltpu.SemaphoreType.DMA((2,)),
            pltpu.SemaphoreType.DMA((COPIES,)),
            pltpu.SemaphoreType.DMA((COPIES,)),
        ],
        compiler_params=pltpu.CompilerParams(
            collective_id=0, has_side_effects=True, vmem_limit_bytes=48 << 20
        ),
        cost_estimate=pl.CostEstimate(flops=2 << 30, bytes_accessed=8 << 20, transcendentals=1 << 20),
    )(adjoint_slab, panel_cols, incoming, inverse_block, panel_rows)
    values = coded[:, :, :256].astype(F32).reshape(2, 4, 32, 8, 128)
    scale = coded[:, :, 256:264].astype(F32).reshape(2, 4, 1, 8, 128) * (1.0 / STEPS)
    steps = jnp.log2(jnp.abs(values)) + HALF
    values = jnp.where(values < 0.0, -steps, steps) * scale
    term = values.reshape(2, 4, 256, 128).transpose(0, 2, 1, 3).reshape(512, 512)
    return gradient, term


def solution(mesh):
    return jax.shard_map(
        on_device,
        mesh=mesh,
        in_specs=(
            P("row", ("col", "depth")),
            P(("col", "depth"), "row"),
            P(("row", "col", "depth"), None),
            P(),
            P(("row", "col", "depth"), None),
        ),
        out_specs=(P(("row", "col", "depth"), None), P()),
        check_vma=False,
    )
```

time: 1170 us -> 86.8 us (0.07)
  waiting for transfers between devices: 1140 us -> 0 us
  Pallas kernels: 0 us -> 77.4 us
  between operations: 13.8 us -> 0.68 us
    reduce_scatter x1 -> x0, waiting for transfers between devices: 825 us -> none  [on_device(): lax.psum_scatter(jnp.dot(adjoint_slab, whole_panel, preferred_element_typ...]
    psum x1 -> x0, waiting for transfers between devices: 273 us -> none  [on_device(): summed = lax.psum(contrib, ('row', 'col', 'depth'))]
    pallas_call x0 -> x1, Pallas kernels: none -> 77.4 us  [on_device(): pl.pallas_call(kernel, name='panel', out_shape=(jax.ShapeDtypeStruct((24,...]
    all_gather x1 -> x0, waiting for transfers between devices: 45.5 us -> none  [on_device(): whole_panel = lax.all_gather(panel_cols, 'row', axis=1, tiled=True)]
  transfers between devices with their start and end apart: 3 -> 0, of which waited for: 3 -> 0; matrix products, arithmetic and copies ran while one was open for 0% -> 0% of each run, Pallas kernels for 0% -> 0%
where the time goes in v1:
time: 86.8 us; the launch traced here: 86.5 us
  Pallas kernels  77.4 us (89%)
  local copies, waits for them, and re-layouts  8.05 us (9%)
    pallas_call x1, Pallas kernels, on_device(): pl.pallas_call(kernel, name='panel', out_shape=(jax.ShapeDtypeStruct((24,...  77.4 us
    unnamed x11, local copies, waits for them, and re-layouts  7.38 us

profile of v1, /device:TPU:1, one launch (start us, length us, event | category | flops | bytes accessed | tf_op | source)
XLA Modules:
  0.0 86.5 jit_solution(13332837739882743872)
XLA Ops:
  0.6 1.1 %copy.8.b_ref = bf16[1024,64]{1,0:T(8,128)(2,1)S(1)} copy(bf16[1024,64]{0,1:T(8,128)(2,1)} %param.6) | data formatting | bytes 262144 | tf_op args[1]
  1.7 0.0 copy-start
  1.7 1.9 %copy-done = bf16[1536,1024]{1,0:T(8,128)(2,1)S(1)} copy-done((bf16[1536,1024]{1,0:T(8,128)(2,1)S(1)}, bf16[1536,1024]{1,0:T(8,128)(2,1)}, u32[]{:S(2)}) %copy-start) | copy-done | bytes 3145752
  3.6 0.0 copy-start.1
  3.6 1.2 %copy-done.1 = f32[512,512]{1,0:T(8,128)S(1)} copy-done((f32[512,512]{1,0:T(8,128)S(1)}, f32[512,512]{1,0:T(8,128)}, u32[]{:S(2)}) %copy-start.1) | copy-done | bytes 1048600
  4.8 0.0 copy-start.2
  4.8 0.8 copy-done.2
  5.6 0.0 copy-start.3
  5.6 0.7 copy-done.3
  6.4 77.4 %panel.1 = (f32[24,512]{1,0:T(8,128)S(1)}, bf16[2,4,272,128]{3,2,1,0:T(8,128)(2,1)S(1)}) custom-call(bf16[1536,1024]{1,0:T(8,128)(2,1)S(1)} %copy-done, bf16[1024,64]{1,0:T(8,128)(2,1)S(1)} %copy.8.b_ref, f32[24,512]{1,0:T(8,128)S(1)} %copy-done.2, f32[512,512]{1,0:T(8,128)S(1)} %copy-done.1, bf16[24,512]{1,0:T(8,128)(2,1)S(1)} %copy-done.3), custom_call_target="tpu_custom_call" | custom-call | flops 2147483648 | bytes 8388608 | tf_op jit(solution)/shard_map/panel/pallas_call | solution.py:223
  83.8 0.3 fusion.4
  84.1 0.7 copy.9
  84.8 1.0 %copy.12 = f32[64,8,4,128]{3,1,2,0:T(8,128)} copy(f32[64,8,4,128]{3,2,1,0:T(4,128)S(1)} %bitcast.9) | data formatting | bytes 2097152
  85.8 0.6 copy.14
  (1 shorter events, 0.0 us)
Async XLA Ops:
  1.7 1.9 %copy-start = (bf16[1536,1024]{1,0:T(8,128)(2,1)S(1)}, bf16[1536,1024]{1,0:T(8,128)(2,1)}, u32[]{:S(2)}) copy-start(bf16[1536,1024]{1,0:T(8,128)(2,1)} %a_hbm.1) | copy-start | bytes 9437188
  3.6 1.2 %copy-start.1 = (f32[512,512]{1,0:T(8,128)S(1)}, f32[512,512]{1,0:T(8,128)}, u32[]{:S(2)}) copy-start(f32[512,512]{1,0:T(8,128)} %inv_hbm.1) | copy-start | bytes 3145732
  4.8 0.8 copy-start.2
  5.6 0.7 copy-start.3

commit v2 on v1

v2 whole, which is shorter than its diff:
```python
import jax
import jax.numpy as jnp
from jax import lax
from jax.experimental import pallas as pl
from jax.experimental.pallas import tpu as pltpu
from jax.sharding import PartitionSpec as P

MESH = pl.DeviceIdType.MESH
F32, BF16 = jnp.float32, jnp.bfloat16
STEPS = 250.0
HALF = 125.0
COPIES = 128
FAR = (4, 3, 5, 2)
NEAR = (6, 1, 7, 0)


def encode(value):
    groups = value.reshape(-1, 8, 128)
    size = jnp.abs(groups)
    scale = jnp.maximum(jnp.max(size, axis=0) * 1.004, 1e-30).astype(BF16)
    power = jnp.exp2(size * (STEPS / scale.astype(F32)) - HALF)
    code = jnp.where(groups < 0.0, -power, power).reshape(value.shape)
    scale = scale.astype(F32)
    return jnp.concatenate([code, scale, scale], axis=0).astype(BF16)


def decode(coded):
    coded = coded.astype(F32)
    rows = coded.shape[0] - 16
    groups = coded[:rows].reshape(-1, 8, 128)
    scale = coded[rows : rows + 8] * (1.0 / STEPS)
    steps = jnp.log2(jnp.abs(groups)) + HALF
    return (jnp.where(groups < 0.0, -steps, steps) * scale).reshape(rows, 128)


def kernel(
    a_hbm, b_hbm, inc_hbm, inv_hbm, p_hbm,
    grad_ref, term_ref,
    a, inv, inc_ref, p_ref, b_all, own, xs, xr, ys, yr, yown, tz, tzr, tx, p_all, p_mat,
    half, half_r, slab, slab_r, zsum, coded, local_sem, send_sem, recv_sem,
):
    row, col, x = lax.axis_index("row"), lax.axis_index("col"), lax.axis_index("depth")
    zl, c = lax.div(row, 2), lax.rem(row, 2)
    y, zh = lax.div(col, 2), lax.rem(col, 2)
    z = zh * 4 + zl

    def at(x=x, y=y, zh=zh, zl=zl, c=c):
        return (zl * 2 + c, y * 2 + zh, x)

    def x_peer(d):
        return at(x=lax.rem(x + d, 4))

    def y_peer(d):
        return at(y=lax.rem(y + d, 8))

    def z_peer(d):
        other = lax.rem(z + d, 8)
        return at(zh=lax.div(other, 4), zl=lax.rem(other, 4))

    sibling = at(c=1 - c)
    z_far = at(zh=1 - zh)

    mine = pl.ds(pl.multiple_of(c * 64, 64), 64)
    loads = []
    for i, (src, dst) in enumerate((
        (p_hbm, p_ref), (b_hbm, b_all.at[zl, mine]), (a_hbm, a), (inc_hbm, inc_ref), (inv_hbm, inv),
    )):
        loads.append(pltpu.make_async_copy(src, dst, local_sem.at[i]))
        loads[-1].start()
    load_p, load_b, load_a, load_inc, load_inv = loads

    barrier = pltpu.get_barrier_semaphore()
    peers = [sibling] + [x_peer(d) for d in range(1, 4)]
    peers += [y_peer(d) for d in range(1, 8)] + [z_peer(d) for d in range(1, 8)]
    for peer in peers:
        pl.semaphore_signal(barrier, inc=1, device_id=peer, device_id_type=MESH)

    pl.semaphore_wait(barrier, len(peers))

    copies = []

    def plan(src, dst, target, send_index=None, recv_index=None):
        i = len(copies)
        copies.append(None)
        return pltpu.make_async_remote_copy(
            src_ref=src, dst_ref=dst,
            send_sem=send_sem.at[i if send_index is None else send_index],
            recv_sem=recv_sem.at[i if recv_index is None else recv_index],
            device_id=target, device_id_type=MESH,
        )

    def send(src, dst, target):
        copy = plan(src, dst, target)
        copy.start()
        copies[-1] = copy
        return copy

    middle = lax.div(lax.rem(zl, 3) + 1, 2)
    two, three = lax.rem(zl + 2, 4), 3 - zl
    chunk = [
        zl,
        zl + 1 - 2 * lax.rem(zl, 2),
        middle * three + (1 - middle) * two,
        middle * two + (1 - middle) * three,
    ]
    slots = [None, 0, 1 + middle, 2 - middle]
    sib = send(b_hbm, b_all.at[zl, mine], sibling)
    first = len(copies)
    line = [None] + [
        plan(b_hbm, b_all.at[zl, mine], at(zl=chunk[k]), first + k - 1, first + slots[k]) for k in range(1, 4)
    ]
    line[1].start()

    @pl.when(middle == 1)
    def _():
        line[2].start()

    load_p.wait()
    wide = jnp.concatenate([p_ref[:, :256].astype(F32), p_ref[:, 256:].astype(F32)], axis=0)
    p_all[x, zh] = wide.astype(BF16)
    p_far = send(p_all.at[x, zh], p_all.at[x, zh], z_far)
    load_a.wait()
    load_b.wait()
    sib.wait_recv()
    x_copies = {}
    y_copies = {}

    def multiply(k):
        for part in range(2):
            acc = lax.dot_general(
                a[part * 768 : part * 768 + 768, :], b_all[chunk[k]], (((1,), (1,)), ((), ())), preferred_element_type=F32
            )
            for yy in range(4):
                for to in range(4):
                    low = yy * 192 + to * 24
                    own[k, to, part * 4 + yy, :24, :] = acc[low : low + 24]
                    own[k, to, part * 4 + yy, 24:, :] = acc[low + 96 : low + 120]
        for part, order in enumerate((FAR, NEAR)):
            for d in (2, 1, 3):
                xs[k, part, d - 1] = encode(blocks_of(k, lax.rem(x + d, 4), order))
                x_copies[k, part, d] = send(xs.at[k, part, d - 1], xr.at[k, part, d - 1], x_peer(d))

    def blocks_of(k, to, order):
        return jnp.concatenate([own[k, to, lax.rem(y + e, 8)] for e in order], axis=0)

    def reduce_x(k, part):
        order = (FAR, NEAR)[part]
        total = blocks_of(k, x, order)
        for d in (1, 3, 2):
            x_copies[k, part, d].wait_recv()
            total = total + decode(xr[k, part, d - 1])
        for j, d in enumerate(order):
            block = total[j * 48 : j * 48 + 48]
            if d == 0:
                yown[k] = block
            else:
                ys[k, d - 1] = encode(block)
                y_copies[k, d] = send(ys.at[k, d - 1], yr.at[k, d - 1], y_peer(d))

    def reduce_y(k):
        total = yown[k]
        for d in (4, 3, 5, 2, 6, 1, 7):
            y_copies[k, d].wait_recv()
            total = total + decode(yr[k, d - 1])
        for h in range(2):
            tz[h, chunk[k]] = total[h * 24 : h * 24 + 24] * -2.0

    multiply(0)

    @pl.when(middle == 1)
    def _():
        line[2].wait_send()
        line[3].start()

    p_far.wait_recv()
    p_copies = [send(p_all.at[x], p_all.at[x], x_peer(d)) for d in range(1, 4)]
    for k in range(1, 4):
        line[k].wait_recv()
        there = b_all.at[chunk[k], mine]
        forward = send(there, there, sibling)
        if k == 1:

            @pl.when(middle == 0)
            def _():
                line[2].start()

        if k >= 2:
            reduce_x(k - 2, 0)
            reduce_x(k - 2, 1)
        forward.wait_recv()
        multiply(k)
        if k == 1:

            @pl.when(middle == 0)
            def _():
                line[2].wait_send()
                line[3].start()

    reduce_x(2, 0)
    reduce_x(2, 1)
    reduce_y(0)
    reduce_y(1)
    for copy in p_copies:
        copy.wait_recv()
    for i in range(4):
        both = p_all[i].astype(F32)
        rows = [jnp.concatenate([both[h, :24], both[h, 24:]], axis=1) for h in range(2)]
        p_mat[i * 48 : i * 48 + 48, :] = jnp.concatenate(rows, axis=0).astype(BF16)
    reduce_x(3, 0)
    reduce_x(3, 1)
    reduce_y(2)
    reduce_y(3)

    far = send(tz.at[1 - zh], tzr, z_far)
    load_inc.wait()
    for i in range(4):
        block = inc_ref[:, i * 128 : i * 128 + 128]
        for h in range(2):
            tx[x, i, h * 24 : h * 24 + 24, :] = tz[h, i] + jnp.where(zh == h, block, 0.0)
    t_copies = []
    for d in range(1, 4):
        to = lax.rem(x + d, 4)
        t_copies.append(send(tx.at[x, to], tx.at[x, to], x_peer(d)))
    for copy in t_copies:
        copy.wait_recv()
    blocks = jnp.concatenate([tx[i, x] for i in range(4)], axis=0)
    high = blocks.astype(BF16)
    rest = blocks - high.astype(F32)
    middle = rest.astype(BF16)
    low = (rest - middle.astype(F32)).astype(BF16)
    contrib = jnp.zeros((512, 128), F32)
    for piece in (low, middle, high):
        contrib = contrib + lax.dot_general(p_mat[...], piece, (((0,), (0,)), ((), ())), preferred_element_type=F32)
    half[...] = contrib.reshape(2, 256, 128)
    swap = send(half.at[1 - c], half_r, sibling)

    load_inv.wait()
    far.wait_recv()
    adjoint = jnp.concatenate([tz[zh, i] + tzr[i] for i in range(4)], axis=1) + inc_ref[...]
    swap.wait_recv()
    slab[...] = (half[c] + half_r[...]).reshape(8, 32, 128)
    s_copies = [None] * 8
    for d in (4, 3, 5, 2, 6, 1, 7):
        s_copies[d] = send(slab.at[lax.rem(y + d, 8)], slab_r.at[d - 1], y_peer(d))
    grad_ref[...] = jnp.dot(adjoint, inv[...], precision=lax.Precision.HIGHEST, preferred_element_type=F32)
    total = slab[y]
    for d in (1, 7, 2, 6, 3, 5, 4):
        s_copies[d].wait_recv()
        total = total + slab_r[d - 1]
    zsum[z] = total
    s_copies = [send(zsum.at[z], zsum.at[z], z_peer(d)) for d in (4, 3, 5, 2, 6, 1, 7)]
    for copy in s_copies:
        copy.wait_recv()
    coded[c, x, y] = encode(jnp.sum(zsum[...], axis=0))

    def spread(source, d):
        piece = coded.at[c, x, source]
        for e in (2, 1, 3):
            x_copies[d, e] = send(piece, piece, x_peer(e))

    piece = coded.at[c, x, y]
    s_copies = [(d, send(piece, piece, y_peer(d))) for d in (4, 3, 5, 2, 6, 1, 7)]
    spread(y, 0)
    for d, copy in reversed(s_copies):
        copy.wait_recv()
        spread(lax.rem(y - d + 8, 8), d)
    last = [send(coded.at[c, x], coded.at[c, x], sibling)]
    for e in (1, 3, 2):
        for d in (0, 7, 1, 6, 2, 5, 3, 4):
            x_copies[d, e].wait_recv()
        source = lax.rem(x - e + 4, 4)
        last.append(send(coded.at[c, source], coded.at[c, source], sibling))
    for copy in last:
        copy.wait_recv()
    term_ref[...] = coded[...]
    line[1].wait_send()
    line[3].wait_send()
    for copy in copies:
        if copy is not None:
            copy.wait_send()


def finish(grad_in, coded, grad_ref, term_ref, term, sems):
    out = [pltpu.make_async_copy(grad_in, grad_ref, sems.at[0])]
    out[0].start()
    for h in range(2):
        for i in range(4):
            for j in range(8):
                term[h, j * 32 : j * 32 + 32, i * 128 : i * 128 + 128] = decode(coded[h, i, j])
        out.append(pltpu.make_async_copy(term.at[h], term_ref.at[h * 256 : h * 256 + 256], sems.at[1 + h]))
        out[-1].start()
    for copy in out:
        copy.wait()


def on_device(adjoint_slab, panel_cols, incoming, inverse_block, panel_rows):
    vmem, hbm = pl.BlockSpec(memory_space=pltpu.VMEM), pl.BlockSpec(memory_space=pltpu.HBM)
    operands = (adjoint_slab, panel_cols.T, incoming, inverse_block, panel_rows)
    gradient, coded = pl.pallas_call(
        kernel,
        name="panel",
        out_shape=(
            jax.ShapeDtypeStruct((24, 512), F32),
            jax.ShapeDtypeStruct((2, 4, 8, 48, 128), BF16),
        ),
        in_specs=[hbm] * 5,
        out_specs=(vmem, vmem),
        scratch_shapes=[
            pltpu.VMEM((1536, 1024), BF16),
            pltpu.VMEM((512, 512), F32),
            pltpu.VMEM((24, 512), F32),
            pltpu.VMEM((24, 512), BF16),
            pltpu.VMEM((4, 128, 1024), BF16),
            pltpu.VMEM((4, 4, 8, 48, 128), F32),
            pltpu.VMEM((4, 2, 3, 208, 128), BF16),
            pltpu.VMEM((4, 2, 3, 208, 128), BF16),
            pltpu.VMEM((4, 7, 64, 128), BF16),
            pltpu.VMEM((4, 7, 64, 128), BF16),
            pltpu.VMEM((4, 48, 128), F32),
            pltpu.VMEM((2, 4, 24, 128), F32),
            pltpu.VMEM((4, 24, 128), F32),
            pltpu.VMEM((4, 4, 48, 128), F32),
            pltpu.VMEM((4, 2, 48, 256), BF16),
            pltpu.VMEM((192, 512), BF16),
            pltpu.VMEM((2, 256, 128), F32),
            pltpu.VMEM((256, 128), F32),
            pltpu.VMEM((8, 32, 128), F32),
            pltpu.VMEM((7, 32, 128), F32),
            pltpu.VMEM((8, 32, 128), F32),
            pltpu.VMEM((2, 4, 8, 48, 128), BF16),
            pltpu.SemaphoreType.DMA((5,)),
            pltpu.SemaphoreType.DMA((COPIES,)),
            pltpu.SemaphoreType.DMA((COPIES,)),
        ],
        compiler_params=pltpu.CompilerParams(
            collective_id=0, has_side_effects=True, vmem_limit_bytes=40 << 20
        ),
        cost_estimate=pl.CostEstimate(flops=2 << 30, bytes_accessed=8 << 20, transcendentals=1 << 20),
    )(*(pltpu.with_memory_space_constraint(array, pltpu.HBM) for array in operands))
    return pl.pallas_call(
        finish,
        name="finish",
        out_shape=(jax.ShapeDtypeStruct((24, 512), F32), jax.ShapeDtypeStruct((512, 512), F32)),
        in_specs=[vmem, vmem],
        out_specs=(hbm, hbm),
        scratch_shapes=[pltpu.VMEM((2, 256, 512), F32), pltpu.SemaphoreType.DMA((3,))],
    )(gradient, coded)


def solution(mesh):
    return jax.shard_map(
        on_device,
        mesh=mesh,
        in_specs=(
            P("row", ("col", "depth")),
            P(("col", "depth"), "row"),
            P(("row", "col", "depth"), None),
            P(),
            P(("row", "col", "depth"), None),
        ),
        out_specs=(P(("row", "col", "depth"), None), P()),
        check_vma=False,
    )
```

time: 86.8 us -> 80.9 us (0.932)
  local copies, waits for them, and re-layouts: 8.05 us -> 1.5 us
  Pallas kernels: 77.4 us -> 78.7 us
    unnamed x11 -> x4, local copies, waits for them, and re-layouts: 7.38 us -> 1.5 us
    pallas_call x0 -> x1, Pallas kernels: none -> 2.3 us  [on_device(): pl.pallas_call(finish, name='finish', out_shape=(jax.ShapeDtypeStruct((24...]
    pallas_call x1, Pallas kernels: 77.4 us -> 76.4 us  [on_device(): pl.pallas_call(kernel, name='panel', out_shape=(jax.ShapeDtypeStruct((24,...]
where the time goes in v2:
time: 80.9 us; the launch traced here: 80.8 us
  Pallas kernels  78.7 us (97%)
  local copies, waits for them, and re-layouts  1.5 us (2%)
    pallas_call x1, Pallas kernels, on_device(): pl.pallas_call(kernel, name='panel', out_shape=(jax.ShapeDtypeStruct((24,...  76.4 us
    pallas_call x1, Pallas kernels, on_device(): pl.pallas_call(finish, name='finish', out_shape=(jax.ShapeDtypeStruct((24...  2.3 us

profile of v2, /device:TPU:1, one launch (start us, length us, event | category | flops | bytes accessed | tf_op | source)
XLA Modules:
  0.0 80.8 jit_solution(2498010066037771643)
XLA Ops:
  0.6 76.4 %panel.1 = (f32[24,512]{1,0:T(8,128)S(1)}, bf16[2,4,8,48,128]{4,3,2,1,0:T(8,128)(2,1)S(1)}) custom-call(bf16[1536,1024]{1,0:T(8,128)(2,1)} %a_hbm.1, bf16[64,1024]{1,0:T(8,128)(2,1)} %bitcast.1, f32[24,512]{1,0:T(8,128)} %inc_hbm.1, f32[512,512]{1,0:T(8,128)} %inv_hbm.1, bf16[24,512]{1,0:T(8,128)(2,1)} %p_hbm.1), custom_call_target="tpu_custom_call" | custom-call | flops 2147483648 | bytes 8388608 | tf_op jit(solution)/shard_map/panel/pallas_call | solution.py:299
  77.0 0.0 copy-start
  77.0 0.9 %copy-done = bf16[2,4,8,48,128]{4,3,2,1,0:T(8,128)(2,1)} copy-done((bf16[2,4,8,48,128]{4,3,2,1,0:T(8,128)(2,1)}, bf16[2,4,8,48,128]{4,3,2,1,0:T(8,128)(2,1)S(1)}, u32[]{:S(2)}) %copy-start) | copy-done | bytes 786456
  77.9 0.0 copy-start.1
  77.9 0.6 copy-done.1
  78.5 2.3 %finish.1 = (f32[24,512]{1,0:T(8,128)}, f32[512,512]{1,0:T(8,128)}) custom-call(f32[24,512]{1,0:T(8,128)} %copy-done.1, bf16[2,4,8,48,128]{4,3,2,1,0:T(8,128)(2,1)} %copy-done), custom_call_target="tpu_custom_call" | custom-call | tf_op jit(solution)/shard_map/finish/pallas_call | solution.py:340
Async XLA Ops:
  77.0 0.9 %copy-start = (bf16[2,4,8,48,128]{4,3,2,1,0:T(8,128)(2,1)}, bf16[2,4,8,48,128]{4,3,2,1,0:T(8,128)(2,1)S(1)}, u32[]{:S(2)}) copy-start(bf16[2,4,8,48,128]{4,3,2,1,0:T(8,128)(2,1)S(1)} %get-tuple-element.5.coded) | copy-start | bytes 2359300
  77.9 0.6 copy-start.1

commit v3 on v2

--- a/solution.py
+++ b/solution.py
@@ -119,6 +119,7 @@
     wide = jnp.concatenate([p_ref[:, :256].astype(F32), p_ref[:, 256:].astype(F32)], axis=0)
     p_all[x, zh] = wide.astype(BF16)
     p_far = send(p_all.at[x, zh], p_all.at[x, zh], z_far)
+    p_copies = [send(p_all.at[x, zh], p_all.at[x, zh], x_peer(d)) for d in range(1, 4)]
     load_a.wait()
     load_b.wait()
     sib.wait_recv()
@@ -172,30 +173,37 @@
         line[2].wait_send()
         line[3].start()
 
-    p_far.wait_recv()
-    p_copies = [send(p_all.at[x], p_all.at[x], x_peer(d)) for d in range(1, 4)]
-    for k in range(1, 4):
+    def arrive(k):
         line[k].wait_recv()
         there = b_all.at[chunk[k], mine]
-        forward = send(there, there, sibling)
-        if k == 1:
-
-            @pl.when(middle == 0)
-            def _():
-                line[2].start()
-
-        if k >= 2:
-            reduce_x(k - 2, 0)
-            reduce_x(k - 2, 1)
-        forward.wait_recv()
-        multiply(k)
-        if k == 1:
-
-            @pl.when(middle == 0)
-            def _():
-                line[2].wait_send()
-                line[3].start()
-
+        return send(there, there, sibling)
+
+    forward = arrive(1)
+
+    @pl.when(middle == 0)
+    def _():
+        line[2].start()
+
+    forward.wait_recv()
+    multiply(1)
+
+    @pl.when(middle == 0)
+    def _():
+        line[2].wait_send()
+        line[3].start()
+
+    forward = arrive(2)
+    reduce_x(0, 0)
+    reduce_x(0, 1)
+    forward.wait_recv()
+    multiply(2)
+    forward = arrive(3)
+    p_far.wait_recv()
+    p_copies += [send(p_all.at[x, 1 - zh], p_all.at[x, 1 - zh], x_peer(d)) for d in range(1, 4)]
+    forward.wait_recv()
+    multiply(3)
+    reduce_x(1, 0)
+    reduce_x(1, 1)
     reduce_x(2, 0)
     reduce_x(2, 1)
     reduce_y(0)
@@ -272,7 +280,11 @@
         last.append(send(coded.at[c, source], coded.at[c, source], sibling))
     for copy in last:
         copy.wait_recv()
-    term_ref[...] = coded[...]
+    for h in range(2):
+        for i in range(4):
+            for j in range(8):
+                low = h * 256 + j * 32
+                term_ref[low : low + 32, i * 128 : i * 128 + 128] = decode(coded[h, i, j])
     line[1].wait_send()
     line[3].wait_send()
     for copy in copies:
@@ -280,28 +292,15 @@
             copy.wait_send()
 
 
-def finish(grad_in, coded, grad_ref, term_ref, term, sems):
-    out = [pltpu.make_async_copy(grad_in, grad_ref, sems.at[0])]
-    out[0].start()
-    for h in range(2):
-        for i in range(4):
-            for j in range(8):
-                term[h, j * 32 : j * 32 + 32, i * 128 : i * 128 + 128] = decode(coded[h, i, j])
-        out.append(pltpu.make_async_copy(term.at[h], term_ref.at[h * 256 : h * 256 + 256], sems.at[1 + h]))
-        out[-1].start()
-    for copy in out:
-        copy.wait()
-
-
 def on_device(adjoint_slab, panel_cols, incoming, inverse_block, panel_rows):
     vmem, hbm = pl.BlockSpec(memory_space=pltpu.VMEM), pl.BlockSpec(memory_space=pltpu.HBM)
     operands = (adjoint_slab, panel_cols.T, incoming, inverse_block, panel_rows)
-    gradient, coded = pl.pallas_call(
+    return pl.pallas_call(
         kernel,
         name="panel",
         out_shape=(
-            jax.ShapeDtypeStruct((24, 512), F32),
-            jax.ShapeDtypeStruct((2, 4, 8, 48, 128), BF16),
+            pltpu.VMEM((24, 512), F32),
+            pltpu.VMEM((512, 512), F32),
         ),
         in_specs=[hbm] * 5,
         out_specs=(vmem, vmem),
@@ -337,15 +336,6 @@
         ),
         cost_estimate=pl.CostEstimate(flops=2 << 30, bytes_accessed=8 << 20, transcendentals=1 << 20),
     )(*(pltpu.with_memory_space_constraint(array, pltpu.HBM) for array in operands))
-    return pl.pallas_call(
-        finish,
-        name="finish",
-        out_shape=(jax.ShapeDtypeStruct((24, 512), F32), jax.ShapeDtypeStruct((512, 512), F32)),
-        in_specs=[vmem, vmem],
-        out_specs=(hbm, hbm),
-        scratch_shapes=[pltpu.VMEM((2, 256, 512), F32), pltpu.SemaphoreType.DMA((3,))],
-    )(gradient, coded)
-
 
 def solution(mesh):
     return jax.shard_map(

time: 80.9 us -> 79.8 us (0.986)
  Pallas kernels: 78.7 us -> 77.5 us
    pallas_call x2 -> x1, Pallas kernels: 78.7 us -> 77.5 us  [on_device(): pl.pallas_call(kernel, name='panel', out_shape=(pltpu.VMEM((24, 512), F32...]
where the time goes in v3:
time: 79.8 us; the launch traced here: 79.7 us
  Pallas kernels  77.5 us (97%)
  local copies, waits for them, and re-layouts  1.59 us (2%)
    pallas_call x1, Pallas kernels, on_device(): pl.pallas_call(kernel, name='panel', out_shape=(pltpu.VMEM((24, 512), F32...  77.5 us

profile of v3, /device:TPU:1, one launch (start us, length us, event | category | flops | bytes accessed | tf_op | source)
XLA Modules:
  0.0 79.7 jit_solution(16134781976481757145)
XLA Ops:
  0.6 77.5 %panel.1 = (f32[24,512]{1,0:T(8,128)S(1)}, f32[512,512]{1,0:T(8,128)S(1)}) custom-call(bf16[1536,1024]{1,0:T(8,128)(2,1)} %a_hbm.1, bf16[64,1024]{1,0:T(8,128)(2,1)} %bitcast.1, f32[24,512]{1,0:T(8,128)} %inc_hbm.1, f32[512,512]{1,0:T(8,128)} %inv_hbm.1, bf16[24,512]{1,0:T(8,128)(2,1)} %p_hbm.1), custom_call_target="tpu_custom_call" | custom-call | flops 2147483648 | bytes 8388608 | tf_op jit(solution)/shard_map/panel/pallas_call | solution.py:298
  78.1 0.6 copy.9
  78.7 1.0 %copy.10 = f32[512,512]{1,0:T(8,128)} copy(f32[512,512]{1,0:T(8,128)S(1)} %get-tuple-element.3) | data formatting | bytes 2097152

commit v4 on v3

--- a/solution.py
+++ b/solution.py
@@ -179,6 +179,8 @@
         return send(there, there, sibling)
 
     forward = arrive(1)
+    p_far.wait_recv()
+    p_copies += [send(p_all.at[x, 1 - zh], p_all.at[x, 1 - zh], x_peer(d)) for d in range(1, 4)]
 
     @pl.when(middle == 0)
     def _():
@@ -198,16 +200,12 @@
     forward.wait_recv()
     multiply(2)
     forward = arrive(3)
-    p_far.wait_recv()
-    p_copies += [send(p_all.at[x, 1 - zh], p_all.at[x, 1 - zh], x_peer(d)) for d in range(1, 4)]
     forward.wait_recv()
     multiply(3)
     reduce_x(1, 0)
     reduce_x(1, 1)
     reduce_x(2, 0)
     reduce_x(2, 1)
-    reduce_y(0)
-    reduce_y(1)
     for copy in p_copies:
         copy.wait_recv()
     for i in range(4):
@@ -216,6 +214,8 @@
         p_mat[i * 48 : i * 48 + 48, :] = jnp.concatenate(rows, axis=0).astype(BF16)
     reduce_x(3, 0)
     reduce_x(3, 1)
+    reduce_y(0)
+    reduce_y(1)
     reduce_y(2)
     reduce_y(3)
 

time: 79.8 us -> 78.6 us (0.985)
  Pallas kernels: 77.5 us -> 76.3 us
    pallas_call x1, Pallas kernels: 77.5 us -> 76.3 us  [on_device(): pl.pallas_call(kernel, name='panel', out_shape=(pltpu.VMEM((24, 512), F32...]
where the time goes in v4:
time: 78.6 us; the launch traced here: 78.5 us
  Pallas kernels  76.3 us (97%)
  local copies, waits for them, and re-layouts  1.59 us (2%)
    pallas_call x1, Pallas kernels, on_device(): pl.pallas_call(kernel, name='panel', out_shape=(pltpu.VMEM((24, 512), F32...  76.3 us
    unnamed x2, local copies, waits for them, and re-layouts  1.59 us

profile of v4, /device:TPU:1, one launch (start us, length us, event | category | flops | bytes accessed | tf_op | source)
XLA Modules:
  0.0 78.5 jit_solution(5188923260703640690)
XLA Ops:
  0.6 76.3 %panel.1 = (f32[24,512]{1,0:T(8,128)S(1)}, f32[512,512]{1,0:T(8,128)S(1)}) custom-call(bf16[1536,1024]{1,0:T(8,128)(2,1)} %a_hbm.1, bf16[64,1024]{1,0:T(8,128)(2,1)} %bitcast.1, f32[24,512]{1,0:T(8,128)} %inc_hbm.1, f32[512,512]{1,0:T(8,128)} %inv_hbm.1, bf16[24,512]{1,0:T(8,128)(2,1)} %p_hbm.1), custom_call_target="tpu_custom_call" | custom-call | flops 2147483648 | bytes 8388608 | tf_op jit(solution)/shard_map/panel/pallas_call | solution.py:298
  76.9 0.6 copy.9
  77.5 1.0 %copy.10 = f32[512,512]{1,0:T(8,128)} copy(f32[512,512]{1,0:T(8,128)S(1)} %get-tuple-element.3) | data formatting | bytes 2097152

commit v5 on v4

--- a/solution.py
+++ b/solution.py
@@ -219,7 +219,6 @@
     reduce_y(2)
     reduce_y(3)
 
-    far = send(tz.at[1 - zh], tzr, z_far)
     load_inc.wait()
     for i in range(4):
         block = inc_ref[:, i * 128 : i * 128 + 128]
@@ -229,6 +228,7 @@
     for d in range(1, 4):
         to = lax.rem(x + d, 4)
         t_copies.append(send(tx.at[x, to], tx.at[x, to], x_peer(d)))
+    far = send(tz.at[1 - zh], tzr, z_far)
     for copy in t_copies:
         copy.wait_recv()
     blocks = jnp.concatenate([tx[i, x] for i in range(4)], axis=0)
@@ -242,14 +242,14 @@
     half[...] = contrib.reshape(2, 256, 128)
     swap = send(half.at[1 - c], half_r, sibling)
 
-    load_inv.wait()
-    far.wait_recv()
-    adjoint = jnp.concatenate([tz[zh, i] + tzr[i] for i in range(4)], axis=1) + inc_ref[...]
     swap.wait_recv()
     slab[...] = (half[c] + half_r[...]).reshape(8, 32, 128)
     s_copies = [None] * 8
     for d in (4, 3, 5, 2, 6, 1, 7):
         s_copies[d] = send(slab.at[lax.rem(y + d, 8)], slab_r.at[d - 1], y_peer(d))
+    load_inv.wait()
+    far.wait_recv()
+    adjoint = jnp.concatenate([tz[zh, i] + tzr[i] for i in range(4)], axis=1) + inc_ref[...]
     grad_ref[...] = jnp.dot(adjoint, inv[...], precision=lax.Precision.HIGHEST, preferred_element_type=F32)
     total = slab[y]
     for d in (1, 7, 2, 6, 3, 5, 4):

time: 78.6 us -> 77.8 us (0.990)
  Pallas kernels: 76.3 us -> 75.5 us
    pallas_call x1, Pallas kernels: 76.3 us -> 75.5 us  [on_device(): pl.pallas_call(kernel, name='panel', out_shape=(pltpu.VMEM((24, 512), F32...]
where the time goes in v5:
time: 77.8 us; the launch traced here: 77.7 us
  Pallas kernels  75.5 us (97%)
  local copies, waits for them, and re-layouts  1.59 us (2%)
    pallas_call x1, Pallas kernels, on_device(): pl.pallas_call(kernel, name='panel', out_shape=(pltpu.VMEM((24, 512), F32...  75.5 us
    unnamed x2, local copies, waits for them, and re-layouts  1.59 us

profile of v5, /device:TPU:1, one launch (start us, length us, event | category | flops | bytes accessed | tf_op | source)
XLA Modules:
  0.0 77.7 jit_solution(9502241005517032035)
XLA Ops:
  0.6 75.5 %panel.1 = (f32[24,512]{1,0:T(8,128)S(1)}, f32[512,512]{1,0:T(8,128)S(1)}) custom-call(bf16[1536,1024]{1,0:T(8,128)(2,1)} %a_hbm.1, bf16[64,1024]{1,0:T(8,128)(2,1)} %bitcast.1, f32[24,512]{1,0:T(8,128)} %inc_hbm.1, f32[512,512]{1,0:T(8,128)} %inv_hbm.1, bf16[24,512]{1,0:T(8,128)(2,1)} %p_hbm.1), custom_call_target="tpu_custom_call" | custom-call | flops 2147483648 | bytes 8388608 | tf_op jit(solution)/shard_map/panel/pallas_call | solution.py:298
  76.1 0.6 copy.9
  76.7 1.0 %copy.10 = f32[512,512]{1,0:T(8,128)} copy(f32[512,512]{1,0:T(8,128)S(1)} %get-tuple-element.3) | data formatting | bytes 2097152

commit v6 on v5

--- a/solution.py
+++ b/solution.py
@@ -206,14 +206,14 @@
     reduce_x(1, 1)
     reduce_x(2, 0)
     reduce_x(2, 1)
+    reduce_x(3, 0)
+    reduce_x(3, 1)
     for copy in p_copies:
         copy.wait_recv()
     for i in range(4):
         both = p_all[i].astype(F32)
         rows = [jnp.concatenate([both[h, :24], both[h, 24:]], axis=1) for h in range(2)]
         p_mat[i * 48 : i * 48 + 48, :] = jnp.concatenate(rows, axis=0).astype(BF16)
-    reduce_x(3, 0)
-    reduce_x(3, 1)
     reduce_y(0)
     reduce_y(1)
     reduce_y(2)

time: 77.8 us -> 77.8 us (level)
  no operation moved by 1% of the time
where the time goes in v6:
time: 77.8 us; the launch traced here: 77.7 us
  Pallas kernels  75.5 us (97%)
  local copies, waits for them, and re-layouts  1.59 us (2%)
    pallas_call x1, Pallas kernels, on_device(): pl.pallas_call(kernel, name='panel', out_shape=(pltpu.VMEM((24, 512), F32...  75.5 us
    unnamed x2, local copies, waits for them, and re-layouts  1.59 us

profile of v6, /device:TPU:1, one launch (start us, length us, event | category | flops | bytes accessed | tf_op | source)
XLA Modules:
  0.0 77.7 jit_solution(10272869055078376005)
XLA Ops:
  0.6 75.5 %panel.1 = (f32[24,512]{1,0:T(8,128)S(1)}, f32[512,512]{1,0:T(8,128)S(1)}) custom-call(bf16[1536,1024]{1,0:T(8,128)(2,1)} %a_hbm.1, bf16[64,1024]{1,0:T(8,128)(2,1)} %bitcast.1, f32[24,512]{1,0:T(8,128)} %inc_hbm.1, f32[512,512]{1,0:T(8,128)} %inv_hbm.1, bf16[24,512]{1,0:T(8,128)(2,1)} %p_hbm.1), custom_call_target="tpu_custom_call" | custom-call | flops 2147483648 | bytes 8388608 | tf_op jit(solution)/shard_map/panel/pallas_call | solution.py:298
  76.1 0.6 copy.9
  76.7 1.0 %copy.10 = f32[512,512]{1,0:T(8,128)} copy(f32[512,512]{1,0:T(8,128)S(1)} %get-tuple-element.3) | data formatting | bytes 2097152
